TPU v7x, 128 devices: a whole 4x4x4 slice. The times are simulated.
128 devices in a mesh: row: 16 (over x, y), col: 8 (over z, core).
Axes of the slice: x: 4, y: 4, z: 4, core: 2. Of those that a mesh axis runs over, the one named last changes fastest.
Arguments:
- panel: bfloat16 [49152, 256], P('row', 'col'), as said below
- trailing: bfloat16 [49152, 16384], P('row', 'col'), may hold values from -6 to 6
- tile_list: int32 [352], P('row'), may hold values from 0 to 23, as said below
Outputs:
- triangle: float32 [256, 256], replicated
- top_rows: float32 [16384, 256], P('col')
- updated: bfloat16 [45056, 16384], P('row', 'col')
Inputs may be any that keep to these rules, and one draw needn't show every extreme that they name: `tile_list`: each aligned block of 22 entries (the entries of one index of row) lists distinct tile numbers of that group's 24 tiles in increasing order and always includes tile 24 - 1. `panel`: the active rows of every row group, and all active rows together, have full column rank with a condition number under 100.
All inputs are finite; a program needn't handle non-finite values.
Results may differ from a plain program's by a relative error of at most 0.0065.
Values may be sent and summed in bfloat16 or wider, within the bound.
A program may use at most 128 MiB of HBM per device.

v0:
```python
import jax
import jax.numpy as jnp
from jax import lax
from jax.sharding import PartitionSpec as P

TILE = 128


def sent_to_all(array, axis):
    copies = jnp.broadcast_to(array, (lax.axis_size(axis), *array.shape))
    return lax.all_to_all(copies, axis, split_axis=0, concat_axis=0, tiled=True)


def laid_out(pieces, dim):
    pieces = jnp.moveaxis(pieces, 0, dim)
    shape = pieces.shape
    return pieces.reshape(*shape[:dim], shape[dim] * shape[dim + 1], *shape[dim + 2 :])


def gather_directly(array, axis, dim):
    pieces = sent_to_all(array, axis)
    return laid_out(pieces, dim)


def taken_together(array, axis):
    everything = sent_to_all(array, axis)
    return jnp.sum(everything.astype(jnp.float32), axis=0)


def pick_tiles(whole, tile_list):
    tiled = whole.reshape(-1, TILE, whole.shape[1])
    return jnp.take(tiled, tile_list, axis=0).reshape(-1, whole.shape[1])


def local(panel, trailing, tile_list):
    panel_full = gather_directly(panel, "col", 1)
    act_panel = pick_tiles(panel_full, tile_list)
    act_trail = pick_tiles(trailing, tile_list)
    local_gram = lax.dot_general(
        act_panel, act_panel, (((0,), (0,)), ((), ())), preferred_element_type=jnp.float32
    )
    gram_matrix = taken_together(local_gram.astype(jnp.bfloat16), "row").astype(jnp.float32)
    lower_factor = jnp.linalg.cholesky(gram_matrix)
    triangle = lower_factor.T
    local_cross = lax.dot_general(
        act_trail, act_panel, (((0,), (0,)), ((), ())), preferred_element_type=jnp.float32
    )
    cross_sum = lax.psum(local_cross, "row")
    top_rows = jax.scipy.linalg.solve_triangular(lower_factor, cross_sum.T, lower=True).T
    coeff = jax.scipy.linalg.solve_triangular(
        lower_factor, top_rows.T, lower=True, trans=1
    ).T.astype(jnp.bfloat16)
    product = lax.dot_general(
        act_panel, coeff, (((1,), (1,)), ((), ())), preferred_element_type=jnp.float32
    )
    updated = (act_trail.astype(jnp.float32) - product).astype(jnp.bfloat16)
    return (triangle, top_rows, updated)


def solution(mesh):
    return jax.shard_map(
        local,
        mesh=mesh,
        in_specs=(P("row", "col"), P("row", "col"), P("row")),
        out_specs=(P(), P("col", None), P("row", "col")),
        check_vma=False,
    )
```

profile of v0, /device:TPU:0, one launch (start us, length us, event | category | flops | bytes accessed | tf_op | source)
XLA Modules:
  0.0 185.2 jit_solution(9979115760256562924)
XLA Ops:
  7.2 0.0 copy-start.2
  7.2 2.3 %broadcast_in_dim.43 = bf16[8,3072,32]{1,2,0:T(8,128)(2,1)} broadcast(bf16[3072,32]{0,1:T(8,128)(2,1)} %param.3), dimensions={1,2} | broadcast | bytes 1769472 | tf_op jit(solution)/shard_map/broadcast_in_dim | solution.py:10
  9.4 5.4 %all-to-all-start = ((bf16[8,3072,32]{1,2,0:T(8,128)(2,1)}), bf16[8,3072,32]{1,2,0:T(8,128)(2,1)S(1)}, u32[]{:S(2)}, u32[]{:S(2)}) async-start(bf16[8,3072,32]{1,2,0:T(8,128)(2,1)} %broadcast_in_dim.43), calls=%async_computation | async-start | bytes 3145728 | tf_op jit(solution)/shard_map/all_to_all | solution.py:11
  14.8 0.0 copy-done.2
  14.9 0.1 broadcast_bitcast_fusion
  14.9 21.5 %all-to-all-done = bf16[8,3072,32]{1,2,0:T(8,128)(2,1)S(1)} async-done(((bf16[8,3072,32]{1,2,0:T(8,128)(2,1)}), bf16[8,3072,32]{1,2,0:T(8,128)(2,1)S(1)}, u32[]{:S(2)}, u32[]{:S(2)}) %all-to-all-start) | async-done | bytes 1572896 | tf_op jit(solution)/shard_map/all_to_all | solution.py:11
  36.4 0.3 copy.25
  36.7 1.1 copy.17
  37.9 0.6 gather_fusion
  38.5 0.9 fusion.7
  39.4 1.5 broadcast_in_dim.46
  40.9 7.0 %all-to-all-start.1 = ((bf16[16,256,256]{2,1,0:T(8,128)(2,1)}), bf16[16,256,256]{2,1,0:T(8,128)(2,1)S(1)}, u32[]{:S(2)}, u32[]{:S(2)}) async-start(bf16[16,256,256]{2,1,0:T(8,128)(2,1)} %broadcast_in_dim.46), calls=%async_computation.1 | async-start | bytes 4194304 | tf_op jit(solution)/shard_map/all_to_all | solution.py:11
  48.0 0.0 all-reduce.3.cloned.1.call-start
  48.0 10.5 %gather_fusion.1 = bf16[22,128,2048]{2,1,0:T(8,128)(2,1)} fusion(bf16[24,128,2048]{2,1,0:T(8,128)(2,1)} %bitcast.64, s32[1024]{0:T(1024)S(1)} %pad_clamp_fusion), kind=kCustom, calls=%fused_computation.1 | custom fusion | bytes 23068760 | tf_op jit(solution)/shard_map/jit(_take)/gather | solution.py:32
  58.5 8.8 %fusion.4 = f32[256,2048]{1,0:T(8,128)} fusion(bf16[22,128,2048]{2,1,0:T(8,128)(2,1)} %gather_fusion.1, pred[22]{0:T(512)(128)(4,1)S(1)} %compare_and_fusion, bf16[22,128,256]{2,1,0:T(8,128)(2,1)S(1)} %gather_fusion), kind=kOutput, calls=%fused_computation.11 | convolution fusion | flops 2959278080 | bytes 15073302 | tf_op jit(solution)/shard_map/dot_general | solution.py:45
  67.4 0.0 all-reduce.3.cloned.1.call-update
  67.4 2.3 %bitcast_select_fusion.1 = bf16[2816,256]{1,0:T(8,128)(2,1)} fusion(bf16[22,128,256]{2,1,0:T(8,128)(2,1)S(1)} %gather_fusion, pred[2816]{0:T(1024)(128)(4,1)S(1)} %broadcast_bitcast_fusion), kind=kLoop, calls=%fused_computation.16 | loop fusion | flops 720896 | bytes 2886400 | tf_op jit(solution)/shard_map/jit(_take)/select_n | solution.py:32
  69.7 8.2 %all-to-all-done.1 = bf16[16,256,256]{2,1,0:T(8,128)(2,1)S(1)} async-done(((bf16[16,256,256]{2,1,0:T(8,128)(2,1)}), bf16[16,256,256]{2,1,0:T(8,128)(2,1)S(1)}, u32[]{:S(2)}, u32[]{:S(2)}) %all-to-all-start.1) | async-done | bytes 2097184 | tf_op jit(solution)/shard_map/all_to_all | solution.py:11
  78.0 0.3 convert_reduce_fusion
  78.2 0.1 copy.19
  78.4 11.7 %cholesky.50 = f32[128,128]{1,0:T(8,128)S(1)} custom-call(f32[128,128]{1,0:T(8,128)S(1)} %cholesky.118), custom_call_target="Cholesky" | custom-call | tf_op jit(solution)/shard_map/jit(cholesky)/cholesky | solution.py:43
  90.2 9.8 %custom-call.18 = f32[1,128,128]{1,2,0:T(8,128)S(1)} custom-call(f32[1,128,128]{2,1,0:T(8,128)S(1)} %get-tuple-element.35), custom_call_target="InvertDiagBlocksLowerTriangular" | custom-call | tf_op jit(solution)/shard_map/jit(cholesky)/cholesky | solution.py:43
  100.0 0.2 constant_dynamic-update-slice_fusion.1
  100.2 0.3 convolution_subtract_fusion.2
  100.5 11.7 %cholesky.105 = f32[128,128]{1,0:T(8,128)S(1)} custom-call(f32[128,128]{1,0:T(8,128)S(1)} %convolution_subtract_fusion.2), custom_call_target="Cholesky" | custom-call | tf_op jit(solution)/shard_map/jit(cholesky)/cholesky | solution.py:43
  112.3 0.6 compare_reduce_fusion
  114.3 0.8 copy.21
  115.1 0.1 triangular_solve.53
  115.2 5.2 %while.1 = (s32[]{:T(128)}, f32[256,256]{1,0:T(8,128)S(1)}, s32[2,2]{1,0:T(2,128)S(1)}, f32[2,128,128]{2,1,0:T(8,128)}, s32[]{:T(128)}) while((s32[]{:T(128)}, f32[256,256]{1,0:T(8,128)S(1)}, s32[2,2]{1,0:T(2,128)S(1)}, f32[2,128,128]{2,1,0:T(8,128)}, s32[]{:T(128)}) %tuple.32), condition=%wide.while_cond, body=%wide.while_body.sunk | while | flops 2 | bytes 132205 | solution.py:49
  115.2 0.6 fusion.37
  115.8 2.0 %bitcast_dynamic-update-slice_fusion.2 = f32[2,128,128]{2,1,0:T(8,128)} fusion(f32[2,128,128]{2,1,0:T(8,128)} %get-tuple-element.79, s32[]{:T(128)S(6)} %copy.32, f32[256,256]{1,0:T(8,128)S(1)} %get-tuple-element.82, s32[]{:T(128)} %bitcast.62, s32[]{:T(128)} %bitcast.63), kind=kLoop, calls=%fused_computation.2.clone.1 | loop fusion | bytes 132100 | tf_op jit(solution)/shard_map/jit(_solve_triangular)/triangular_solve
  117.8 0.6 fusion.37
  118.3 2.0 %bitcast_dynamic-update-slice_fusion.2 = f32[2,128,128]{2,1,0:T(8,128)} fusion(f32[2,128,128]{2,1,0:T(8,128)} %get-tuple-element.79, s32[]{:T(128)S(6)} %copy.32, f32[256,256]{1,0:T(8,128)S(1)} %get-tuple-element.82, s32[]{:T(128)} %bitcast.62, s32[]{:T(128)} %bitcast.63), kind=kLoop, calls=%fused_computation.2.clone.1 | loop fusion | bytes 132100 | tf_op jit(solution)/shard_map/jit(_solve_triangular)/triangular_solve
  120.4 20.5 %custom-call.19 = f32[2,128,128]{1,2,0:T(8,128)S(1)} custom-call(f32[2,128,128]{2,1,0:T(8,128)} %get-tuple-element.10), custom_call_target="InvertDiagBlocksLowerTriangular" | custom-call | tf_op jit(solution)/shard_map/jit(_solve_triangular)/triangular_solve | solution.py:49
  140.9 16.8 %all-reduce.3.cloned.1.call-done = f32[256,2048]{1,0:T(8,128)} async-done(((f32[256,2048]{1,0:T(8,128)}), f32[256,2048]{1,0:T(8,128)}) %all-reduce.3.cloned.1.call-update) | async-done | bytes 2097168 | tf_op jit(solution)/shard_map/psum | solution.py:48
  157.7 0.0 copy-start
  157.7 2.4 %fusion.8 = f32[128,2048]{1,0:T(8,128)S(1)} fusion(f32[256,2048]{1,0:T(8,128)} %all-reduce.3.cloned.1.call-done, f32[2,128,128]{1,2,0:T(8,128)S(1)} %custom-call.19), kind=kOutput, calls=%fused_computation.21 | convolution fusion | flops 402653184 | bytes 2162688 | tf_op jit(solution)/shard_map/jit(_solve_triangular)/triangular_solve | solution.py:49
  160.1 0.0 copy-done
  160.1 1.0 convolution_subtract_fusion.1
  161.1 1.0 fusion.20
  162.2 1.8 fusion.27
  164.0 0.1 maximum_bitcast_fusion
  164.1 1.1 convolution_subtract_fusion
  165.2 1.8 convolution_convert_fusion
  167.0 0.0 copy-start.1
  167.0 1.8 copy.22
  168.9 0.0 copy-done.1
  168.9 9.5 %subtract_convert_fusion = bf16[2816,2048]{1,0:T(8,128)(2,1)} fusion(bf16[22,128,2048]{2,1,0:T(8,128)(2,1)} %gather_fusion.1, pred[2816]{0:T(1024)(128)(4,1)S(1)} %broadcast_bitcast_fusion, bf16[2816,256]{1,0:T(8,128)(2,1)S(1)} %copy-done.1, bf16[128,2048]{1,0:T(8,128)(2,1)} %get-tuple-element.38, bf16[128,2048]{1,0:T(8,128)(2,1)} %convolution_convert_fusion), kind=kOutput, calls=%fused_computation.4 | convolution fusion | flops 2977955840 | bytes 25561856 | tf_op jit(solution)/shard_map/dot_general | solution.py:53
  (13 shorter events, 0.2 us)
Async XLA Ops:
  7.2 7.7 %copy-start.2 = (s32[22]{0:T(128)S(1)}, s32[22]{0:T(128)}, u32[]{:S(2)}) copy-start(s32[22]{0:T(128)} %param.5) | copy-start | bytes 268
  9.4 27.0 %all-to-all-start = ((bf16[8,3072,32]{1,2,0:T(8,128)(2,1)}), bf16[8,3072,32]{1,2,0:T(8,128)(2,1)S(1)}, u32[]{:S(2)}, u32[]{:S(2)}) async-start(bf16[8,3072,32]{1,2,0:T(8,128)(2,1)} %broadcast_in_dim.43), calls=%async_computation | async-start | bytes 3145728 | tf_op jit(solution)/shard_map/all_to_all | solution.py:11
  40.9 37.0 %all-to-all-start.1 = ((bf16[16,256,256]{2,1,0:T(8,128)(2,1)}), bf16[16,256,256]{2,1,0:T(8,128)(2,1)S(1)}, u32[]{:S(2)}, u32[]{:S(2)}) async-start(bf16[16,256,256]{2,1,0:T(8,128)(2,1)} %broadcast_in_dim.46), calls=%async_computation.1 | async-start | bytes 4194304 | tf_op jit(solution)/shard_map/all_to_all | solution.py:11
  48.0 109.7 %all-reduce.3.cloned.1.call-start = ((), (), s32[]{:S(2)}) async-start(), calls=%async_computation.2 | async-start | bytes 4194304 | tf_op jit(solution)/shard_map/psum | solution.py:48
  157.7 2.4 %copy-start = (f32[256,2048]{1,0:T(8,128)S(1)}, f32[256,2048]{1,0:T(8,128)}, u32[]{:S(2)}) copy-start(f32[256,2048]{1,0:T(8,128)} %all-reduce.3.cloned.1.call-done) | copy-start | bytes 6291460
  167.0 1.8 copy-start.1
Sparse Core Ops, SparseCore 0:
  67.5 90.1 all-reduce.2
where the time goes:
time: 186 us; the launch traced here: 185 us
  other arithmetic  57.3 us (31%)
  waiting for transfers between devices  46.5 us (25%)
  matrix products  28.8 us (15%)
  local copies, waits for them, and re-layouts  24.5 us (13%)
  between operations  15.5 us (8%)
  starting transfers between devices  12.5 us (7%)
    another operation x6, other arithmetic, local(): lower_factor = jnp.linalg.cholesky(gram_matrix)  34 us
    all_to_all x2, waiting for transfers between devices, sent_to_all(): return lax.all_to_all(copies, axis, split_axis=0, concat_axis=0, tiled=True)  29.7 us
    another operation x3, other arithmetic, local(): jax.scipy.linalg.solve_triangular(lower_factor, cross_sum.T, lower=True)  20.5 us
    psum x1, waiting for transfers between devices, local(): cross_sum = lax.psum(local_cross, 'row')  16.8 us
    all_to_all x2, starting transfers between devices, sent_to_all(): return lax.all_to_all(copies, axis, split_axis=0, concat_axis=0, tiled=True)  12.4 us
    gather x2, local copies, waits for them, and re-layouts, pick_tiles(): return jnp.take(tiled, tile_list, axis=0).reshape(-1, whole.shape[1])  11.1 us
    dot_general x1, matrix products, local(): lax.dot_general(act_panel, coeff, (((1,), (1,)), ((), ())), preferred_ele...  9.49 us
    dot_general x1, matrix products, local(): lax.dot_general(act_trail, act_panel, (((0,), (0,)), ((), ())), preferred...  8.84 us
  transfers between devices with their start and end apart: 3, of which 3 were waited for; matrix products, arithmetic and copies ran while one was open for 45% of the time, Pallas kernels for 0%

commit v1 on v0

--- a/solution.py
+++ b/solution.py
@@ -45,7 +45,11 @@
     local_cross = lax.dot_general(
         act_trail, act_panel, (((0,), (0,)), ((), ())), preferred_element_type=jnp.float32
     )
-    cross_sum = lax.psum(local_cross, "row")
+    cross_sum = local_cross
+    for hop in (1, 2, 4, 8):
+        cross_sum = cross_sum + lax.ppermute(
+            cross_sum, "row", [(dev, dev ^ hop) for dev in range(16)]
+        )
     top_rows = jax.scipy.linalg.solve_triangular(lower_factor, cross_sum.T, lower=True).T
     coeff = jax.scipy.linalg.solve_triangular(
         lower_factor, top_rows.T, lower=True, trans=1

time: 186 us -> 298 us (1.60)
  waiting for transfers between devices: 46.5 us -> 155 us
  between operations: 15.5 us -> 2.18 us
  starting transfers between devices: 12.5 us -> 21.9 us
  other arithmetic: 57.3 us -> 64.6 us
  matrix products: 28.8 us -> 24.5 us
  local copies, waits for them, and re-layouts: 24.5 us -> 27.8 us
    ppermute x0 -> x4, waiting for transfers between devices: none -> 126 us  [local(): lax.ppermute(cross_sum, 'row', [(dev, dev ^ hop) for dev in range(16)])]
    psum x1 -> x0, waiting for transfers between devices: 16.8 us -> none  [local(): cross_sum = lax.psum(local_cross, 'row')]
    ppermute x0 -> x4, starting transfers between devices: none -> 9.77 us  [local(): lax.ppermute(cross_sum, 'row', [(dev, dev ^ hop) for dev in range(16)])]
  transfers between devices with their start and end apart: 3 -> 6, of which waited for: 3 -> 5; matrix products, arithmetic and copies ran while one was open for 45% -> 27% of each run, Pallas kernels for 0% -> 0%
where the time goes in v1:
time: 298 us; the launch traced here: 296 us
  waiting for transfers between devices  155 us (52%)
  other arithmetic  64.6 us (22%)
  local copies, waits for them, and re-layouts  27.8 us (9%)
  matrix products  24.5 us (8%)
  starting transfers between devices  21.9 us (7%)
    ppermute x4, waiting for transfers between devices, local(): lax.ppermute(cross_sum, 'row', [(dev, dev ^ hop) for dev in range(16)])  126 us
    another operation x6, other arithmetic, local(): lower_factor = jnp.linalg.cholesky(gram_matrix)  34 us
    all_to_all x2, waiting for transfers between devices, sent_to_all(): return lax.all_to_all(copies, axis, split_axis=0, concat_axis=0, tiled=True)  28.8 us
    another operation x3, other arithmetic, local(): jax.scipy.linalg.solve_triangular(lower_factor, cross_sum.T, lower=True)  20.5 us
    all_to_all x2, starting transfers between devices, sent_to_all(): return lax.all_to_all(copies, axis, split_axis=0, concat_axis=0, tiled=True)  12.2 us
    gather x2, local copies, waits for them, and re-layouts, pick_tiles(): return jnp.take(tiled, tile_list, axis=0).reshape(-1, whole.shape[1])  11.1 us
    ppermute x4, starting transfers between devices, local(): lax.ppermute(cross_sum, 'row', [(dev, dev ^ hop) for dev in range(16)])  9.77 us
    dot_general x1, matrix products, local(): lax.dot_general(act_panel, coeff, (((1,), (1,)), ((), ())), preferred_ele...  9.27 us
  transfers between devices with their start and end apart: 6, of which 5 were waited for; matrix products, arithmetic and copies ran while one was open for 27% of the time, Pallas kernels for 0%

profile of v1, /device:TPU:0, one launch (start us, length us, event | category | flops | bytes accessed | tf_op | source)
XLA Modules:
  0.0 295.5 jit_solution(7376495794511246197)
XLA Ops:
  0.6 0.0 copy-start.3
  0.6 2.3 broadcast_in_dim.43
  2.9 5.4 %all-to-all-start = ((bf16[8,3072,32]{1,2,0:T(8,128)(2,1)}), bf16[8,3072,32]{1,2,0:T(8,128)(2,1)S(1)}, u32[]{:S(2)}, u32[]{:S(2)}) async-start(bf16[8,3072,32]{1,2,0:T(8,128)(2,1)} %broadcast_in_dim.43), calls=%async_computation | async-start | bytes 3145728 | tf_op jit(solution)/shard_map/all_to_all | solution.py:11
  8.3 0.0 copy-done.3
  8.3 10.5 %gather_fusion.1 = bf16[22,128,2048]{2,1,0:T(8,128)(2,1)} fusion(bf16[24,128,2048]{2,1,0:T(8,128)(2,1)} %bitcast.65, s32[1024]{0:T(1024)S(1)} %pad_clamp_fusion), kind=kCustom, calls=%fused_computation.1 | custom fusion | bytes 23068760 | tf_op jit(solution)/shard_map/jit(_take)/gather | solution.py:32
  18.8 11.1 %all-to-all-done = bf16[8,3072,32]{1,2,0:T(8,128)(2,1)S(1)} async-done(((bf16[8,3072,32]{1,2,0:T(8,128)(2,1)}), bf16[8,3072,32]{1,2,0:T(8,128)(2,1)S(1)}, u32[]{:S(2)}, u32[]{:S(2)}) %all-to-all-start) | async-done | bytes 1572896 | tf_op jit(solution)/shard_map/all_to_all | solution.py:11
  29.9 1.5 copy.36
  31.3 2.1 copy.26
  33.5 0.6 gather_fusion
  34.1 6.8 %fusion.4 = f32[2048,256]{1,0:T(8,128)S(1)} fusion(bf16[22,128,2048]{2,1,0:T(8,128)(2,1)} %gather_fusion.1, pred[22]{0:T(512)(128)(4,1)S(1)} %compare_and_fusion, bf16[22,128,256]{2,1,0:T(8,128)(2,1)S(1)} %gather_fusion), kind=kOutput, calls=%fused_computation.11 | convolution fusion | flops 2959278080 | bytes 15073302 | tf_op jit(solution)/shard_map/dot_general | solution.py:45
  41.0 1.7 collective-permute-start
  42.6 45.6 %collective-permute-done = f32[2048,256]{1,0:T(8,128)S(1)} collective-permute-done((f32[2048,256]{1,0:T(8,128)S(1)}, f32[2048,256]{1,0:T(8,128)S(1)}, u32[]{:S(2)}, u32[]{:S(2)}) %collective-permute-start) | collective-permute-done | bytes 2097184 | tf_op jit(solution)/shard_map/ppermute | solution.py:50
  88.2 0.3 add.46
  88.5 3.3 %collective-permute-start.1 = (f32[2048,256]{1,0:T(8,128)S(1)}, f32[2048,256]{1,0:T(8,128)S(1)}, u32[]{:S(2)}, u32[]{:S(2)}) collective-permute-start(f32[2048,256]{1,0:T(8,128)S(1)} %add.46), channel_id=1, source_target_pairs={{0,16},{8,24},{16,0},{24,8},{32,48},{40,56},{48,32},{56,40},{64,80... | collective-permute-start | bytes 6291464 | tf_op jit(solution)/shard_map/ppermute | solution.py:50
  91.8 44.6 %collective-permute-done.1 = f32[2048,256]{1,0:T(8,128)S(1)} collective-permute-done((f32[2048,256]{1,0:T(8,128)S(1)}, f32[2048,256]{1,0:T(8,128)S(1)}, u32[]{:S(2)}, u32[]{:S(2)}) %collective-permute-start.1) | collective-permute-done | bytes 2097184 | tf_op jit(solution)/shard_map/ppermute | solution.py:50
  136.4 0.3 add.47
  136.6 0.0 copy-start
  136.6 1.6 collective-permute-start.2
  138.2 0.9 fusion.7
  139.1 1.5 broadcast_in_dim.46
  140.6 0.0 copy-done
  140.6 6.8 %all-to-all-start.1 = ((bf16[16,256,256]{2,1,0:T(8,128)(2,1)}), bf16[16,256,256]{2,1,0:T(8,128)(2,1)}, u32[]{:S(2)}, u32[]{:S(2)}) async-start(bf16[16,256,256]{2,1,0:T(8,128)(2,1)} %broadcast_in_dim.46), calls=%async_computation.1 | async-start | bytes 4194304 | tf_op jit(solution)/shard_map/all_to_all | solution.py:11
  147.4 0.0 copy-start.1
  147.4 0.1 broadcast_bitcast_fusion
  147.5 2.3 bitcast_select_fusion.1
  149.8 35.6 %collective-permute-done.2 = f32[2048,256]{1,0:T(8,128)} collective-permute-done((f32[2048,256]{1,0:T(8,128)S(1)}, f32[2048,256]{1,0:T(8,128)}, u32[]{:S(2)}, u32[]{:S(2)}) %collective-permute-start.2) | collective-permute-done | bytes 2097184 | tf_op jit(solution)/shard_map/ppermute | solution.py:50
  185.4 0.0 copy-done.1
  185.4 1.9 add.48
  187.3 3.3 %collective-permute-start.3 = (f32[2048,256]{1,0:T(8,128)S(1)}, f32[2048,256]{1,0:T(8,128)}, u32[]{:S(2)}, u32[]{:S(2)}) collective-permute-start(f32[2048,256]{1,0:T(8,128)S(1)} %add.48), channel_id=1, source_target_pairs={{0,64},{8,72},{16,80},{24,88},{32,96},{40,104},{48,112},{56,120},{... | collective-permute-start | bytes 6291464 | tf_op jit(solution)/shard_map/ppermute | solution.py:50
  190.5 17.7 %all-to-all-done.1 = bf16[16,256,256]{2,1,0:T(8,128)(2,1)} async-done(((bf16[16,256,256]{2,1,0:T(8,128)(2,1)}), bf16[16,256,256]{2,1,0:T(8,128)(2,1)}, u32[]{:S(2)}, u32[]{:S(2)}) %all-to-all-start.1) | async-done | bytes 2097184 | tf_op jit(solution)/shard_map/all_to_all | solution.py:11
  208.2 1.9 convert_reduce_fusion
  210.1 0.1 copy.28
  210.3 11.7 %cholesky.50 = f32[128,128]{1,0:T(8,128)S(1)} custom-call(f32[128,128]{1,0:T(8,128)S(1)} %cholesky.118), custom_call_target="Cholesky" | custom-call | tf_op jit(solution)/shard_map/jit(cholesky)/cholesky | solution.py:43
  222.1 9.8 %custom-call.18 = f32[1,128,128]{1,2,0:T(8,128)S(1)} custom-call(f32[1,128,128]{2,1,0:T(8,128)S(1)} %get-tuple-element.38), custom_call_target="InvertDiagBlocksLowerTriangular" | custom-call | tf_op jit(solution)/shard_map/jit(cholesky)/cholesky | solution.py:43
  231.9 0.2 constant_dynamic-update-slice_fusion.1
  232.1 0.3 convolution_subtract_fusion.1
  232.4 11.7 %cholesky.105 = f32[128,128]{1,0:T(8,128)S(1)} custom-call(f32[128,128]{1,0:T(8,128)S(1)} %convolution_subtract_fusion.1), custom_call_target="Cholesky" | custom-call | tf_op jit(solution)/shard_map/jit(cholesky)/cholesky | solution.py:43
  244.2 0.6 compare_reduce_fusion
  246.2 0.8 copy.31
  247.0 0.1 triangular_solve.53
  247.1 5.2 %while.1 = (s32[]{:T(128)}, f32[256,256]{1,0:T(8,128)S(1)}, s32[2,2]{1,0:T(2,128)S(1)}, f32[2,128,128]{2,1,0:T(8,128)}, s32[]{:T(128)}) while((s32[]{:T(128)}, f32[256,256]{1,0:T(8,128)S(1)}, s32[2,2]{1,0:T(2,128)S(1)}, f32[2,128,128]{2,1,0:T(8,128)}, s32[]{:T(128)}) %tuple.33), condition=%wide.while_cond, body=%wide.while_body.sunk | while | flops 2 | bytes 132205 | solution.py:53
  247.1 0.6 fusion.37
  247.7 2.0 bitcast_dynamic-update-slice_fusion.2
  249.7 0.6 fusion.37
  250.2 2.0 bitcast_dynamic-update-slice_fusion.2
  252.3 20.5 %custom-call.19 = f32[2,128,128]{1,2,0:T(8,128)S(1)} custom-call(f32[2,128,128]{2,1,0:T(8,128)} %get-tuple-element.10), custom_call_target="InvertDiagBlocksLowerTriangular" | custom-call | tf_op jit(solution)/shard_map/jit(_solve_triangular)/triangular_solve | solution.py:53
  272.7 0.0 collective-permute-done.3
  272.8 1.9 add_bitcast_fusion
  274.6 1.1 fusion.9
  275.7 1.8 fusion.22
  277.5 1.1 fusion.8
  278.6 1.0 fusion.28
  279.7 1.5 maximum_bitcast_fusion
  281.2 1.0 convolution_subtract_fusion
  282.3 1.0 convolution_convert_fusion
  283.3 0.0 copy-start.2
  283.3 3.0 %copy.32 = f32[2048,256]{1,0:T(8,128)} copy(f32[2048,256]{0,1:T(8,128)} %maximum_bitcast_fusion) | data formatting | bytes 4194304
  286.3 0.0 copy-done.2
  286.3 9.3 %subtract_convert_fusion = bf16[2816,2048]{1,0:T(8,128)(2,1)} fusion(bf16[22,128,2048]{2,1,0:T(8,128)(2,1)} %gather_fusion.1, pred[2816]{0:T(1024)(128)(4,1)S(1)} %broadcast_bitcast_fusion, bf16[2816,256]{1,0:T(8,128)(2,1)S(1)} %copy-done.2, bf16[128,2048]{1,0:T(8,128)(2,1)S(1)} %get-tuple-element.41, bf16[128,2048]{1,0:T(8,128)(2,1)S(1)} %convolution_convert_fusion), kind=kOutput, calls=%fused_computation.4 | convolution fusion | flops 2977955840 | bytes 25561856 | tf_op jit(solution)/shard_map/dot_general | solution.py:57
  (13 shorter events, 0.2 us)
Async XLA Ops:
  0.6 7.7 %copy-start.3 = (s32[22]{0:T(128)S(1)}, s32[22]{0:T(128)}, u32[]{:S(2)}) copy-start(s32[22]{0:T(128)} %param.5) | copy-start | bytes 268
  2.9 27.0 %all-to-all-start = ((bf16[8,3072,32]{1,2,0:T(8,128)(2,1)}), bf16[8,3072,32]{1,2,0:T(8,128)(2,1)S(1)}, u32[]{:S(2)}, u32[]{:S(2)}) async-start(bf16[8,3072,32]{1,2,0:T(8,128)(2,1)} %broadcast_in_dim.43), calls=%async_computation | async-start | bytes 3145728 | tf_op jit(solution)/shard_map/all_to_all | solution.py:11
  41.0 47.3 %collective-permute-start = (f32[2048,256]{1,0:T(8,128)S(1)}, f32[2048,256]{1,0:T(8,128)S(1)}, u32[]{:S(2)}, u32[]{:S(2)}) collective-permute-start(f32[2048,256]{1,0:T(8,128)S(1)} %fusion.4), channel_id=1, source_target_pairs={{0,8},{8,0},{16,24},{24,16},{32,40},{40,32},{48,56},{56,48},{64,72... | collective-permute-start | bytes 6291464 | tf_op jit(solution)/shard_map/ppermute | solution.py:50
  88.5 47.9 %collective-permute-start.1 = (f32[2048,256]{1,0:T(8,128)S(1)}, f32[2048,256]{1,0:T(8,128)S(1)}, u32[]{:S(2)}, u32[]{:S(2)}) collective-permute-start(f32[2048,256]{1,0:T(8,128)S(1)} %add.46), channel_id=1, source_target_pairs={{0,16},{8,24},{16,0},{24,8},{32,48},{40,56},{48,32},{56,40},{64,80... | collective-permute-start | bytes 6291464 | tf_op jit(solution)/shard_map/ppermute | solution.py:50
  136.6 4.0 %copy-start = (f32[2048,256]{1,0:T(8,128)}, f32[2048,256]{1,0:T(8,128)S(1)}, u32[]{:S(2)}) copy-start(f32[2048,256]{1,0:T(8,128)S(1)} %add.47) | copy-start | bytes 6291460
  136.6 48.8 %collective-permute-start.2 = (f32[2048,256]{1,0:T(8,128)S(1)}, f32[2048,256]{1,0:T(8,128)}, u32[]{:S(2)}, u32[]{:S(2)}) collective-permute-start(f32[2048,256]{1,0:T(8,128)S(1)} %add.47), channel_id=1, source_target_pairs={{0,32},{8,40},{16,48},{24,56},{32,0},{40,8},{48,16},{56,24},{64,96... | collective-permute-start | bytes 6291464 | tf_op jit(solution)/shard_map/ppermute | solution.py:50
  140.6 67.6 %all-to-all-start.1 = ((bf16[16,256,256]{2,1,0:T(8,128)(2,1)}), bf16[16,256,256]{2,1,0:T(8,128)(2,1)}, u32[]{:S(2)}, u32[]{:S(2)}) async-start(bf16[16,256,256]{2,1,0:T(8,128)(2,1)} %broadcast_in_dim.46), calls=%async_computation.1 | async-start | bytes 4194304 | tf_op jit(solution)/shard_map/all_to_all | solution.py:11
  147.4 38.0 %copy-start.1 = (f32[2048,256]{1,0:T(8,128)S(1)}, f32[2048,256]{1,0:T(8,128)}, u32[]{:S(2)}) copy-start(f32[2048,256]{1,0:T(8,128)} %copy-done) | copy-start | bytes 6291460
  187.3 85.5 %collective-permute-start.3 = (f32[2048,256]{1,0:T(8,128)S(1)}, f32[2048,256]{1,0:T(8,128)}, u32[]{:S(2)}, u32[]{:S(2)}) collective-permute-start(f32[2048,256]{1,0:T(8,128)S(1)} %add.48), channel_id=1, source_target_pairs={{0,64},{8,72},{16,80},{24,88},{32,96},{40,104},{48,112},{56,120},{... | collective-permute-start | bytes 6291464 | tf_op jit(solution)/shard_map/ppermute | solution.py:50
  283.3 3.0 %copy-start.2 = (bf16[2816,256]{1,0:T(8,128)(2,1)S(1)}, bf16[2816,256]{1,0:T(8,128)(2,1)}, u32[]{:S(2)}) copy-start(bf16[2816,256]{1,0:T(8,128)(2,1)} %bitcast_select_fusion.1) | copy-start | bytes 4325380
